TPU v7x, 128 devices: a whole 4x4x4 slice. The times are simulated.
128 devices in a mesh: ep: 4 (over z_hi, core), fsdp: 32 (over y, z_lo, x).
Axes of the slice: x: 4, y: 4, z: 4 (z_hi: 2, z_lo: 2; z = z_hi * 2 + z_lo), core: 2. Of those that a mesh axis runs over, the one named last changes fastest.
Arguments:
- gate_weight: bfloat16 [32, 4096, 1536], P('ep', 'fsdp'), may hold values from -0.09375 to 0.09375
- up_weight: bfloat16 [32, 4096, 1536], P('ep', 'fsdp'), may hold values from -0.09375 to 0.09375
- down_weight: bfloat16 [32, 4096, 1536], P('ep', 'fsdp'), may hold values from -0.09375 to 0.09375
- model_factors: bfloat16 [32, 3, 64, 4096], P('ep', None, None, 'fsdp'), may hold values from -0.09375 to 0.09375
- hidden_factors: bfloat16 [32, 3, 64, 1536], P('ep', None, 'fsdp'), may hold values from -0.75 to 0.75
- active: int32 [32], P('ep'), may hold values 0 or 1
- expert_rollout_slot: int32 [32], replicated, may hold values from 0 to 31, each once
Outputs:
- quantized: bfloat16 [32, 3, 4096, 1536], P('fsdp', None, None, 'ep')
- block_scales: bfloat16 [32, 3, 32, 12], P('fsdp', None, None, 'ep')
Inputs may be any that keep to these rules, and one draw needn't show every extreme that they name: `expert_rollout_slot`: each slot number appears exactly once; slot s belongs to rollout owner s.
All inputs are finite; a program needn't handle non-finite values. No bound on the sum of `active` on one device may be relied on, other than what follows from the above.
Results may differ from a plain program's by a relative error of at most 0.004.
Values may be sent and summed in bfloat16 or wider, within the bound.
A program may use at most 128 MiB of HBM per device.

v0:
```python
import jax
import jax.numpy as jnp
from jax import lax
from jax.sharding import PartitionSpec as P

BLK = 128


ADAPTER_SCALE = 2.0


def quantize(merged_weight):
    lead = merged_weight.shape[:-2]
    rows = merged_weight.shape[-2]
    cols = merged_weight.shape[-1]
    blocks = merged_weight.reshape(lead + (rows // BLK, BLK, cols // BLK, BLK))
    block_max = jnp.max(jnp.abs(blocks), axis=(-3, -1))
    scales = (block_max + 1e-06).astype(jnp.bfloat16)
    widened_values = lax.optimization_barrier(scales).astype(jnp.float32)
    values = (
        (blocks / widened_values[..., :, None, :, None])
        .reshape(merged_weight.shape)
        .astype(jnp.bfloat16)
    )
    return (values, scales)


def on_device(
    gate_weight, up_weight, down_weight, model_factors, hidden_factors, active, expert_rollout_slot
):
    stacked = jnp.stack([gate_weight, up_weight, down_weight], axis=1)
    adapter_update = jnp.einsum(
        "gprd,gprf->gpdf",
        model_factors,
        lax.all_gather(hidden_factors, "fsdp", axis=2, tiled=True),
        preferred_element_type=jnp.float32,
    )
    weight_factor = ADAPTER_SCALE * active.astype(jnp.float32)
    merged_weight = (
        stacked.astype(jnp.float32) + weight_factor[:, None, None, None] * adapter_update
    )
    count = expert_rollout_slot.shape[0]
    slots = jnp.arange(count, dtype=jnp.int32)
    source = jnp.sum(
        jnp.where(expert_rollout_slot[None, :] == slots[:, None], slots[None, :], 0), axis=1
    )
    values, scales = quantize(merged_weight)
    col_values, col_scales = (
        lax.all_to_all(values, "ep", split_axis=3, concat_axis=0, tiled=True),
        lax.all_to_all(scales, "ep", split_axis=3, concat_axis=0, tiled=True),
    )
    ordered_values = jnp.take(col_values, source, axis=0)
    ordered_scales = jnp.take(col_scales, source, axis=0)
    quantized, block_scales = (
        lax.all_to_all(ordered_values, "fsdp", split_axis=0, concat_axis=2, tiled=True),
        lax.all_to_all(ordered_scales, "fsdp", split_axis=0, concat_axis=2, tiled=True),
    )
    return (quantized, block_scales)


def solution(mesh):
    placed = (
        P("ep", "fsdp", None),
        P("ep", "fsdp", None),
        P("ep", "fsdp", None),
        P("ep", None, None, "fsdp"),
        P("ep", None, "fsdp", None),
        P("ep"),
        P(),
    )
    return jax.shard_map(
        on_device,
        mesh=mesh,
        in_specs=placed,
        out_specs=(P("fsdp", None, None, "ep"), P("fsdp", None, None, "ep")),
        check_vma=False,
    )
```

profile of v0, /device:TPU:3, one launch (start us, length us, event | category | flops | bytes accessed | tf_op | source)
XLA Modules:
  0.0 527.2 jit_solution(17657351648358208946)
XLA Ops:
  7.2 0.0 copy-start
  7.2 0.0 all-gather.2.cloned.1.call-start
  7.2 1.6 copy.59
  8.9 0.0 all-gather.2.cloned.1.call-update
  8.9 0.7 convert_multiply_fusion
  9.5 142.7 %all-gather.2.cloned.1.call-done = bf16[8,3,64,1536]{3,0,1,2:T(8,128)(2,1)} async-done(((bf16[8,3,2,1536]{3,0,1,2:T(8,128)(2,1)}), bf16[8,3,64,1536]{3,0,1,2:T(8,128)(2,1)}) %all-gather.2.cloned.1.call-update) | async-done | bytes 4718608 | tf_op jit(solution)/shard_map/all_gather | solution.py:35
  152.2 0.0 copy-done
  152.2 12.3 %abs_reduce_fusion = (f32[8,3,1536]{2,1,0:T(4,128)S(1)}, f32[8,3,128,1536]{3,2,1,0:T(8,128)}) fusion(f32[8]{0:T(128)S(1)} %convert_multiply_fusion, bf16[8,1,128,1536]{3,2,1,0:T(8,128)(2,1)} %bitcast.42, bf16[8,1,128,1536]{3,2,1,0:T(8,128)(2,1)} %bitcast.44, bf16[8,1,128,1536]{3,2,1,0:T(8,128)(2,1)} %bitcast.46, bf16[8,3,64,128]{3,2,1,0:T(8,128)(2,1)S(1)} %copy-done, ...), kind=kOutput, calls=%fused_computation.3 | convolution fusion | flops 636973056 | bytes 33570848 | tf_op jit(solution)/shard_map/gprd,gprf->gpdf/dot_general | solution.py:32
  164.5 0.1 copy.61
  164.6 0.1 reduce_max.18
  164.7 0.7 copy.67
  165.5 0.1 div.21
  165.6 0.1 copy.62
  165.7 23.2 %all-to-all-start.2 = ((bf16[8,3,1,12]{0,1,2,3:T(4,128)(2,1)}), bf16[8,3,1,12]{0,1,2,3:T(4,128)(2,1)S(1)}, u32[]{:S(2)}, u32[]{:S(2)}) async-start(bf16[8,3,1,12]{0,1,2,3:T(4,128)(2,1)} %copy.67), calls=%async_computation.2 | async-start | bytes 24576 | tf_op jit(solution)/shard_map/all_to_all | solution.py:50
  188.9 13.1 %divide_convert_fusion = bf16[8,3,128,1536]{3,2,1,0:T(8,128)(2,1)} fusion(f32[8,3,128,1536]{3,2,1,0:T(8,128)} %get-tuple-element.15, f32[8,3,1536]{2,1,0:T(4,128)S(1)} %copy.62, f32[8]{0:T(128)S(1)} %convert_multiply_fusion, bf16[8,1,128,1536]{3,2,1,0:T(8,128)(2,1)S(1)} %bitcast.43, bf16[8,1,128,1536]{3,2,1,0:T(8,128)(2,1)} %bitcast.45, ...), kind=kLoop, calls=%fused_computation.2 | loop fusion | flops 33030144 | bytes 37896224 | tf_op jit(solution)/shard_map/convert_element_type | solution.py:23
  202.0 13.2 %copy.63 = bf16[8,3,128,1536]{2,0,1,3:T(8,128)(2,1)} copy(bf16[8,3,128,1536]{3,2,1,0:T(8,128)(2,1)} %divide_convert_fusion) | data formatting | bytes 18874368 | tf_op jit(solution)/shard_map/convert_element_type | solution.py:23
  215.2 0.0 all-to-all-done.2
  215.2 6.0 %all-to-all-start = ((bf16[8,3,128,1536]{2,0,1,3:T(8,128)(2,1)}), bf16[8,3,128,1536]{2,0,1,3:T(8,128)(2,1)}, u32[]{:S(2)}, u32[]{:S(2)}) async-start(bf16[8,3,128,1536]{2,0,1,3:T(8,128)(2,1)} %copy.63), calls=%async_computation | async-start | bytes 18874368 | tf_op jit(solution)/shard_map/all_to_all | solution.py:49
  221.2 0.1 select_reduce_fusion
  221.3 0.2 copy.73
  221.5 0.6 gather_fusion.1
  222.1 0.7 fusion.2
  222.8 103.4 %all-to-all-done = bf16[8,3,128,1536]{2,0,1,3:T(8,128)(2,1)} async-done(((bf16[8,3,128,1536]{2,0,1,3:T(8,128)(2,1)}), bf16[8,3,128,1536]{2,0,1,3:T(8,128)(2,1)}, u32[]{:S(2)}, u32[]{:S(2)}) %all-to-all-start) | async-done | bytes 9437216 | tf_op jit(solution)/shard_map/all_to_all | solution.py:49
  326.2 6.5 %all-to-all-start.3 = ((bf16[32,3,1,3]{3,1,2,0:T(4,128)(2,1)}), bf16[32,3,1,3]{3,1,2,0:T(4,128)(2,1)S(1)}, u32[]{:S(2)}, u32[]{:S(2)}) async-start(bf16[32,3,1,3]{3,1,2,0:T(4,128)(2,1)} %fusion.2), calls=%async_computation.3 | async-start | bytes 65536 | tf_op jit(solution)/shard_map/all_to_all | solution.py:56
  332.7 12.8 %copy.65 = bf16[4,8,3,128,384]{4,3,2,1,0:T(8,128)(2,1)} copy(bf16[4,8,3,128,384]{3,1,2,4,0:T(8,128)(2,1)} %bitcast.7) | data formatting | bytes 18874368 | tf_op jit(solution)/shard_map/all_to_all | solution.py:49
  345.5 9.6 %gather_fusion = bf16[32,3,128,384]{3,2,1,0:T(8,128)(2,1)} fusion(bf16[32,3,128,384]{3,2,1,0:T(8,128)(2,1)} %bitcast.40, s32[1024]{0:T(1024)S(1)} %pad_clamp_fusion), kind=kCustom, calls=%fused_computation | custom fusion | bytes 18874496 | tf_op jit(solution)/shard_map/jit(_take)/gather | solution.py:52
  355.1 8.5 %broadcast_select_fusion = bf16[32,3,128,384]{3,2,1,0:T(8,128)(2,1)} fusion(bf16[32,3,128,384]{3,2,1,0:T(8,128)(2,1)} %gather_fusion, pred[32]{0:T(512)(128)(4,1)S(1)} %compare_and_fusion), kind=kLoop, calls=%fused_computation.6 | loop fusion | flops 4718592 | bytes 18874400 | tf_op jit(solution)/shard_map/jit(_take)/select_n | solution.py:52
  363.6 0.0 all-to-all-done.3
  363.6 7.8 %all-to-all-start.1 = ((bf16[32,3,128,384]{3,2,1,0:T(8,128)(2,1)}), bf16[32,3,128,384]{3,2,1,0:T(8,128)(2,1)}, u32[]{:S(2)}, u32[]{:S(2)}) async-start(bf16[32,3,128,384]{3,2,1,0:T(8,128)(2,1)} %broadcast_select_fusion), calls=%async_computation.1 | async-start | bytes 18874368 | tf_op jit(solution)/shard_map/all_to_all | solution.py:55
  371.4 0.7 copy.71
  372.1 139.0 %all-to-all-done.1 = bf16[32,3,128,384]{3,2,1,0:T(8,128)(2,1)} async-done(((bf16[32,3,128,384]{3,2,1,0:T(8,128)(2,1)}), bf16[32,3,128,384]{3,2,1,0:T(8,128)(2,1)}, u32[]{:S(2)}, u32[]{:S(2)}) %all-to-all-start.1) | async-done | bytes 9437216 | tf_op jit(solution)/shard_map/all_to_all | solution.py:55
  511.1 9.3 %copy.66 = bf16[1,3,32,128,384]{4,3,2,1,0:T(8,128)(2,1)} copy(bf16[1,3,32,128,384]{4,3,1,2,0:T(8,128)(2,1)} %bitcast.12) | data formatting | bytes 18874368 | tf_op jit(solution)/shard_map/all_to_all | solution.py:55
  (13 shorter events, 0.1 us)
Async XLA Ops:
  7.2 145.1 %copy-start = (bf16[8,3,64,128]{3,2,1,0:T(8,128)(2,1)S(1)}, bf16[8,3,64,128]{3,2,1,0:T(8,128)(2,1)}, u32[]{:S(2)}) copy-start(bf16[8,3,64,128]{3,2,1,0:T(8,128)(2,1)} %param.10) | copy-start | bytes 1179652
  7.2 145.1 %all-gather.2.cloned.1.call-start = ((), (), s32[]{:S(2)}) async-start(), calls=%async_computation.4 | async-start | bytes 4866048 | tf_op jit(solution)/shard_map/all_gather | solution.py:35
  152.2 36.7 %copy-start.2 = (bf16[8,128,1536]{2,1,0:T(8,128)(2,1)S(1)}, bf16[8,128,1536]{2,1,0:T(8,128)(2,1)}, u32[]{:S(2)}) copy-start(bf16[8,128,1536]{2,1,0:T(8,128)(2,1)} %param.9) | copy-start | bytes 9437188
  165.7 49.5 %all-to-all-start.2 = ((bf16[8,3,1,12]{0,1,2,3:T(4,128)(2,1)}), bf16[8,3,1,12]{0,1,2,3:T(4,128)(2,1)S(1)}, u32[]{:S(2)}, u32[]{:S(2)}) async-start(bf16[8,3,1,12]{0,1,2,3:T(4,128)(2,1)} %copy.67), calls=%async_computation.2 | async-start | bytes 24576 | tf_op jit(solution)/shard_map/all_to_all | solution.py:50
  215.2 6.0 %copy-start.3 = (s32[32]{0:T(128)S(1)}, s32[32]{0:T(128)}, u32[]{:S(2)}) copy-start(s32[32]{0:T(128)} %param.13) | copy-start | bytes 388
  215.2 111.0 %all-to-all-start = ((bf16[8,3,128,1536]{2,0,1,3:T(8,128)(2,1)}), bf16[8,3,128,1536]{2,0,1,3:T(8,128)(2,1)}, u32[]{:S(2)}, u32[]{:S(2)}) async-start(bf16[8,3,128,1536]{2,0,1,3:T(8,128)(2,1)} %copy.63), calls=%async_computation | async-start | bytes 18874368 | tf_op jit(solution)/shard_map/all_to_all | solution.py:49
  326.2 37.4 %all-to-all-start.3 = ((bf16[32,3,1,3]{3,1,2,0:T(4,128)(2,1)}), bf16[32,3,1,3]{3,1,2,0:T(4,128)(2,1)S(1)}, u32[]{:S(2)}, u32[]{:S(2)}) async-start(bf16[32,3,1,3]{3,1,2,0:T(4,128)(2,1)} %fusion.2), calls=%async_computation.3 | async-start | bytes 65536 | tf_op jit(solution)/shard_map/all_to_all | solution.py:56
  363.6 147.4 %all-to-all-start.1 = ((bf16[32,3,128,384]{3,2,1,0:T(8,128)(2,1)}), bf16[32,3,128,384]{3,2,1,0:T(8,128)(2,1)}, u32[]{:S(2)}, u32[]{:S(2)}) async-start(bf16[32,3,128,384]{3,2,1,0:T(8,128)(2,1)} %broadcast_select_fusion), calls=%async_computation.1 | async-start | bytes 18874368 | tf_op jit(solution)/shard_map/all_to_all | solution.py:55
  511.1 9.3 %copy-start.1 = (bf16[8,3,64,128]{3,2,1,0:T(8,128)(2,1)S(1)}, bf16[8,3,64,128]{3,2,1,0:T(8,128)(2,1)}, u32[]{:S(2)}) copy-start(bf16[8,3,64,128]{3,2,1,0:T(8,128)(2,1)} %param.10) | copy-start | bytes 1179652
Sparse Core Ops, SparseCore 0:
  10.2 141.9 all-gather.1
where the time goes:
time: 530 us; the launch traced here: 527 us
  waiting for transfers between devices  385 us (73%)
  local copies, waits for them, and re-layouts  49 us (9%)
  starting transfers between devices  43.5 us (8%)
  other arithmetic  23.3 us (4%)
  between operations  14.1 us (3%)
  matrix products  12.3 us (2%)
    all_gather x1, waiting for transfers between devices, on_device(): lax.all_gather(hidden_factors, 'fsdp', axis=2, tiled=True)  143 us
    all_to_all x1, waiting for transfers between devices, on_device(): lax.all_to_all(ordered_values, 'fsdp', split_axis=0, concat_axis=2, tiled...  139 us
    all_to_all x1, waiting for transfers between devices, on_device(): lax.all_to_all(values, 'ep', split_axis=3, concat_axis=0, tiled=True)  103 us
    all_to_all x1, starting transfers between devices, on_device(): lax.all_to_all(scales, 'ep', split_axis=3, concat_axis=0, tiled=True)  23.2 us
    convert_element_type x1, local copies, waits for them, and re-layouts, quantize(): values = (blocks / widened_values[..., :, None, :, None]).reshape(merged_...  13.2 us
    convert_element_type x1, other arithmetic, quantize(): values = (blocks / widened_values[..., :, None, :, None]).reshape(merged_...  13.1 us
    all_to_all x1, local copies, waits for them, and re-layouts, on_device(): lax.all_to_all(values, 'ep', split_axis=3, concat_axis=0, tiled=True)  12.8 us
    dot_general x1, matrix products, on_device(): jnp.einsum('gprd,gprf->gpdf', model_factors, lax.all_gather(hidden_factor...  12.3 us
  transfers between devices with their start and end apart: 5, of which 3 were waited for; matrix products, arithmetic and copies ran while one was open for 11% of the time, Pallas kernels for 0%

commit v1 on v0

v1 whole, which is shorter than its diff:
```python
import jax
import jax.numpy as jnp
from jax import lax
from jax.experimental import pallas as pl
from jax.experimental.pallas import tpu as pltpu
from jax.sharding import PartitionSpec as P

BLK = 128
ADAPTER_SCALE = 2.0
EP = 4
OWNERS = 32
LOCAL = 8
EXPERTS = EP * LOCAL
MATS = 3
RANK = 64
COLS = 384
NCB = COLS // BLK
MF_ROWS = MATS * RANK
HF_ROWS = 32
AUX_ROWS = MF_ROWS + HF_ROWS
CHUNKS = tuple((p, cb, 1) for p in range(MATS) for cb in range(NCB))
LAG = 1
MESH = pl.DeviceIdType.MESH


def kernel(source, gate, up, down, mf, hfp, out, scales_out, *scratch):
    n = len(CHUNKS)
    a_bufs, b_bufs, l_bufs = scratch[: n + 1], scratch[n + 1 : 2 * n + 2], scratch[2 * n + 2 : 3 * n + 3]
    o_bufs, (hf_all, a_send, a_recv, b_send, b_recv, o_sem) = scratch[3 * n + 3 : 4 * n + 3], scratch[4 * n + 3 :]
    weights = (gate, up, down)

    k, j = lax.axis_index("ep"), lax.axis_index("fsdp")
    h = k // 2
    y, l, x = j // 8, (j // 4) % 2, j % 4
    flip = 4 - 8 * l

    def partner(d):
        k2 = (k + d) % EP
        dh = k2 // 2 - h
        return k2, j + dh * dh * flip

    def owner(o):
        return ((y + o // 8) % 4) * 8 + ((l + (o // 4) % 2) % 2) * 4 + (x + o % 4) % 4

    barrier = pltpu.get_barrier_semaphore()
    for d in range(1, EP):
        pl.semaphore_signal(barrier, inc=1, device_id=partner(d), device_id_type=MESH)

    @pl.loop(1, OWNERS)
    def _(o):
        pl.semaphore_signal(barrier, inc=1, device_id=(k, owner(o)), device_id_type=MESH)

    pl.semaphore_wait(barrier, EP - 1 + OWNERS - 1)

    mine = pl.ds(k * LOCAL, LOCAL)

    def a_pairs(c, k2):
        if c == n:
            return (
                (mf, a_bufs[n].at[mine, pl.ds(0, MF_ROWS), :]),
                (hfp.at[:, k2], a_bufs[n].at[mine, pl.ds(MF_ROWS, HF_ROWS), :]),
            )
        p, cb, m = CHUNKS[c]
        columns = pl.ds(pl.multiple_of(k2 * COLS + cb * BLK, BLK), m * BLK)
        return ((weights[p].at[:, :, columns], a_bufs[c].at[mine]),)

    def a_start(c):
        for d in range(1, EP):
            k2, j2 = partner(d)
            for src, dst in a_pairs(c, k2):
                pltpu.make_async_remote_copy(
                    src_ref=src, dst_ref=dst, send_sem=a_send.at[c], recv_sem=a_recv.at[c],
                    device_id=(k2, j2), device_id_type=MESH,
                ).start()
        for src, dst in a_pairs(c, k):
            pltpu.make_async_copy(src, dst, a_recv.at[c]).start()

    def b_start(c):
        a, b, land = a_bufs[c], b_bufs[c], l_bufs[c]

        @pl.loop(0, OWNERS)
        def _(s):
            b[s] = a[source[s]]

        @pl.loop(1, OWNERS)
        def _(o):
            s = owner(o)
            pltpu.make_async_remote_copy(
                src_ref=b.at[s], dst_ref=land.at[j], send_sem=b_send.at[c], recv_sem=b_recv.at[c],
                device_id=(k, s), device_id_type=MESH,
            ).start()

        pltpu.make_async_copy(b.at[j], land.at[j], b_recv.at[c]).start()

    order = (n,) + tuple(range(n))
    for c in order:
        a_start(c)

    crossed = source[j] // (2 * LOCAL) - h
    crossed = crossed * crossed

    def factors():
        pltpu.make_async_copy(l_bufs[n], l_bufs[n], b_recv.at[n]).wait()
        packed = l_bufs[n][:, MF_ROWS:, :].reshape(OWNERS * HF_ROWS, BLK)
        row = lax.broadcasted_iota(jnp.int32, (RANK, OWNERS * HF_ROWS), 0)
        col = lax.broadcasted_iota(jnp.int32, (RANK, OWNERS * HF_ROWS), 1)
        holder = row // 2
        holder = holder + crossed * (4 - 8 * ((holder // 4) % 2))
        first = holder * HF_ROWS + (row % 2) * NCB
        for p in range(MATS):
            for cb in range(NCB):
                pick = jnp.where(col == first + (p * 2 * NCB + cb), 1.0, 0.0).astype(jnp.bfloat16)
                hf_all[p, :, cb * BLK : (cb + 1) * BLK] = jnp.dot(
                    pick, packed, preferred_element_type=jnp.float32
                ).astype(jnp.bfloat16)

    def compute(c):
        p, cb0, m = CHUNKS[c]
        pltpu.make_async_copy(l_bufs[c], l_bufs[c], b_recv.at[c]).wait()
        land, aux, o_buf = l_bufs[c], l_bufs[n], o_bufs[c]

        @pl.loop(0, OWNERS, unroll=4)
        def _(i):
            held = i + crossed * (4 - 8 * ((i // 4) % 2))
            delta = lax.dot_general(
                aux[held, p * RANK : (p + 1) * RANK, :],
                hf_all[p, :, cb0 * BLK : (cb0 + m) * BLK],
                (((0,), (0,)), ((), ())),
                preferred_element_type=jnp.float32,
            )
            merged = land[held].astype(jnp.float32) + delta
            for q in range(m):
                block = merged[:, q * BLK : (q + 1) * BLK]
                most = jnp.max(jnp.max(jnp.abs(block), axis=0, keepdims=True), axis=1, keepdims=True)
                scale = (most + 1e-6).astype(jnp.bfloat16).astype(jnp.float32)
                o_buf[i, :, q * BLK : (q + 1) * BLK] = (block * (1.0 / scale)).astype(jnp.bfloat16)
                scales_out[p * NCB + cb0 + q, pl.ds(i, 1), :] = jnp.broadcast_to(scale, (1, BLK))

        pltpu.make_async_copy(o_buf, out.at[p, :, :, pl.ds(cb0 * BLK, m * BLK)], o_sem.at[c]).start()

    done = 0
    for at, c in enumerate(order):
        pltpu.make_async_copy(a_bufs[c], a_bufs[c], a_recv.at[c]).wait()
        b_start(c)
        while done < at - LAG:
            if done == 0:
                factors()
            compute(done)
            done += 1
    while done < n:
        if done == 0:
            factors()
        compute(done)
        done += 1

    for c in range(n + 1):
        given = a_bufs[c].at[pl.ds(0, EXPERTS - LOCAL)]
        pltpu.make_async_copy(given, given, a_send.at[c]).wait()
        given = b_bufs[c].at[pl.ds(0, OWNERS - 1)]
        pltpu.make_async_copy(given, given, b_send.at[c]).wait()
    for c, (p, cb0, m) in enumerate(CHUNKS):
        pltpu.make_async_copy(o_bufs[c], out.at[p, :, :, pl.ds(cb0 * BLK, m * BLK)], o_sem.at[c]).wait()


def on_device(
    gate_weight, up_weight, down_weight, model_factors, hidden_factors, active, expert_rollout_slot
):
    n = len(CHUNKS)
    slots = jnp.arange(EXPERTS, dtype=jnp.int32)
    source = jnp.sum(
        jnp.where(expert_rollout_slot[None, :] == slots[:, None], slots[None, :], 0), axis=1
    ).astype(jnp.int32)
    mf = model_factors.reshape(LOCAL, MF_ROWS, BLK)
    factor = (ADAPTER_SCALE * active.astype(jnp.float32)).astype(jnp.bfloat16)
    hf = hidden_factors * factor[:, None, None, None]
    hfp = hf.reshape(LOCAL, MATS * 2, EP, NCB, BLK).transpose(0, 2, 1, 3, 4)
    hfp = hfp.reshape(LOCAL, EP, MATS * 2 * NCB, BLK)
    hfp = jnp.pad(hfp, ((0, 0), (0, 0), (0, HF_ROWS - MATS * 2 * NCB), (0, 0)))

    def bufs():
        shapes = [(OWNERS, BLK, m * BLK) for _, _, m in CHUNKS] + [(OWNERS, AUX_ROWS, BLK)]
        return [pltpu.VMEM(shape, jnp.bfloat16) for shape in shapes]

    quantized, scales = pl.pallas_call(
        kernel,
        out_shape=(
            jax.ShapeDtypeStruct((MATS, OWNERS, BLK, COLS), jnp.bfloat16),
            jax.ShapeDtypeStruct((MATS * NCB, OWNERS, BLK), jnp.float32),
        ),
        in_specs=[pl.BlockSpec(memory_space=pltpu.SMEM)] + [pl.BlockSpec(memory_space=pl.ANY)] * 5,
        out_specs=(pl.BlockSpec(memory_space=pl.ANY), pl.BlockSpec(memory_space=pltpu.VMEM)),
        scratch_shapes=bufs() + bufs() + bufs() + bufs()[:n] + [
            pltpu.VMEM((MATS, RANK, COLS), jnp.bfloat16),
            pltpu.SemaphoreType.DMA((n + 1,)),
            pltpu.SemaphoreType.DMA((n + 1,)),
            pltpu.SemaphoreType.DMA((n + 1,)),
            pltpu.SemaphoreType.DMA((n + 1,)),
            pltpu.SemaphoreType.DMA((n,)),
        ],
        compiler_params=pltpu.CompilerParams(
            collective_id=0, has_side_effects=True, vmem_limit_bytes=60 * 1024 * 1024
        ),
    )(source, gate_weight, up_weight, down_weight, mf, hfp)
    quantized = quantized.reshape(1, MATS, OWNERS * BLK, COLS)
    block_scales = scales[:, :, 0].reshape(MATS, NCB, OWNERS).transpose(0, 2, 1)
    return quantized, block_scales[None].astype(jnp.bfloat16)


def solution(mesh):
    placed = (
        P("ep", "fsdp", None),
        P("ep", "fsdp", None),
        P("ep", "fsdp", None),
        P("ep", None, None, "fsdp"),
        P("ep", None, "fsdp", None),
        P("ep"),
        P(),
    )
    return jax.shard_map(
        on_device,
        mesh=mesh,
        in_specs=placed,
        out_specs=(P("fsdp", None, None, "ep"), P("fsdp", None, None, "ep")),
        check_vma=False,
    )
```

time: 530 us -> 180 us (0.34)
  waiting for transfers between devices: 385 us -> 0 us
  Pallas kernels: 0 us -> 164 us
  starting transfers between devices: 43.5 us -> 0 us
  local copies, waits for them, and re-layouts: 49 us -> 10.9 us
  other arithmetic: 23.3 us -> 3.04 us
  between operations: 14.1 us -> 0.68 us
  matrix products: 12.3 us -> 0 us
    all_to_all x4 -> x0, waiting for transfers between devices: 242 us -> none  [the longest x1 139 us: on_device(): lax.all_to_all(ordered_values, 'fsdp', split_axis=0, concat_axis=2, tiled...]
    pallas_call x0 -> x1, Pallas kernels: none -> 164 us  [on_device(): pl.pallas_call(kernel, out_shape=(jax.ShapeDtypeStruct((MATS, OWNERS, BLK...]
    all_gather x1 -> x0, waiting for transfers between devices: 143 us -> none  [on_device(): lax.all_gather(hidden_factors, 'fsdp', axis=2, tiled=True)]
    all_to_all x4 -> x0, starting transfers between devices: 43.5 us -> none  [the longest x1 23.2 us: on_device(): lax.all_to_all(scales, 'ep', split_axis=3, concat_axis=0, tiled=True)]
    all_to_all x3 -> x0, local copies, waits for them, and re-layouts: 22.3 us -> none  [the longest x1 12.8 us: on_device(): lax.all_to_all(values, 'ep', split_axis=3, concat_axis=0, tiled=True)]
    convert_element_type x2 -> x1, local copies, waits for them, and re-layouts: 13.9 us -> 0.6 us  [on_device(): return (quantized, block_scales[None].astype(jnp.bfloat16))]
    convert_element_type x2 -> x1, other arithmetic: 13.1 us -> 0.66 us  [on_device(): factor = (ADAPTER_SCALE * active.astype(jnp.float32)).astype(jnp.bfloat16)]
    dot_general x1 -> x0, matrix products: 12.3 us -> none  [on_device(): jnp.einsum('gprd,gprf->gpdf', model_factors, lax.all_gather(hidden_factor...]
  transfers between devices with their start and end apart: 5 -> 0, of which waited for: 3 -> 0; matrix products, arithmetic and copies ran while one was open for 11% -> 0% of each run, Pallas kernels for 0% -> 0%
where the time goes in v1:
time: 180 us; the launch traced here: 178 us
  Pallas kernels  164 us (91%)
  local copies, waits for them, and re-layouts  10.9 us (6%)
  other arithmetic  3.04 us (2%)
    pallas_call x1, Pallas kernels, on_device(): pl.pallas_call(kernel, out_shape=(jax.ShapeDtypeStruct((MATS, OWNERS, BLK...  164 us
    unnamed x1, local copies, waits for them, and re-layouts  8.36 us

profile of v1, /device:TPU:3, one launch (start us, length us, event | category | flops | bytes accessed | tf_op | source)
XLA Modules:
  0.0 178.3 jit_solution(2667825625992025624)
XLA Ops:
  0.6 0.7 multiply_convert_fusion
  1.3 1.3 select_reduce_fusion.source
  2.6 1.1 broadcast_multiply_fusion
  3.7 0.1 reshape.21
  3.9 0.7 pad.4.hfp
  4.6 163.7 %shard_map.86 = (bf16[3,32,128,384]{3,2,1,0:T(8,128)(2,1)}, f32[9,32,128]{2,1,0:T(8,128)}) custom-call(s32[32]{0:T(128)} %select_reduce_fusion.source, bf16[8,128,1536]{2,1,0:T(8,128)(2,1)} %gate.1, bf16[8,128,1536]{2,1,0:T(8,128)(2,1)} %up.1, bf16[8,128,1536]{2,1,0:T(8,128)(2,1)} %down.1, bf16[8,192,128]{2,1,0:T(8,128)(2,1)} %bitcast.14, ...), custom_call_target="tpu_custom_call" | custom-call | tf_op jit(solution)/shard_map/pallas_call | solution.py:184
  168.3 1.0 fusion
  169.4 0.6 convert_element_type.20
  170.0 8.4 %copy.17 = bf16[1,3,4096,384]{3,2,1,0:T(8,128)(2,1)} copy(bf16[1,3,4096,384]{3,2,1,0:T(8,128)(2,1)} %bitcast.11) | data formatting | bytes 18874368
  (3 shorter events, 0.1 us)

commit v2 on v1

v2 whole, which is shorter than its diff:
```python
import jax
import jax.numpy as jnp
from jax import lax
from jax.experimental import pallas as pl
from jax.experimental.pallas import tpu as pltpu
from jax.sharding import PartitionSpec as P

BLK = 128
ADAPTER_SCALE = 2
EP = 4
OWNERS = 32
LOCAL = 8
EXPERTS = EP * LOCAL
MATS = 3
RANK = 64
HALF = RANK // 2
COLS = 384
NCB = COLS // BLK
BLOCKS = MATS * NCB
ROWS = ((64, 64),) + ((128,),) * 7 + ((64, 64),)
PIECES = tuple(
    (b, sum(cut[:i]), rows) for b, cut in enumerate(ROWS) for i, rows in enumerate(cut)
)
AUX = len(PIECES)
AUX_AT = 2
ORDER = tuple(range(AUX_AT)) + (AUX,) + tuple(range(AUX_AT, AUX))
LAG = 2
STEP = 13
MESH = pl.DeviceIdType.MESH


def kernel(active, slot, gate, up, down, mf, hf, out, scales_out, *scratch):
    n = AUX + 1
    a_bufs, b_bufs, l_bufs = scratch[:n], scratch[n : 2 * n], scratch[2 * n : 3 * n]
    (hf_in, hf_wide, hf_rows, sibling, hf_all, source,
     a_send, a_recv, b_send, b_recv, c_send, c_recv, in_sem) = scratch[3 * n :]
    weights = (gate, up, down)

    k, j = lax.axis_index("ep"), lax.axis_index("fsdp")
    h, core = k // 2, k % 2
    y, l, x = j // 8, (j // 4) % 2, j % 4
    flip = 4 - 8 * l

    def partner(d):
        k2 = (k + d) % EP
        dh = k2 // 2 - h
        return k2, j + dh * dh * flip

    def owner(o):
        o = (o * STEP) % OWNERS
        return ((y + o // 8) % 4) * 8 + ((l + (o // 4) % 2) % 2) * 4 + (x + o % 4) % 4

    barrier = pltpu.get_barrier_semaphore()
    for d in range(1, EP):
        pl.semaphore_signal(barrier, inc=1, device_id=partner(d), device_id_type=MESH)

    @pl.loop(1, OWNERS)
    def _(o):
        pl.semaphore_signal(barrier, inc=1, device_id=(k, owner(o)), device_id_type=MESH)

    hf_copy = pltpu.make_async_copy(hf, hf_in, in_sem)
    hf_copy.start()
    pl.semaphore_wait(barrier, EP - 1 + OWNERS - 1)

    mine = pl.ds(k * LOCAL, LOCAL)

    def a_pairs(c, k2):
        if c == AUX:
            return (
                (mf.at[:, :, pl.ds((k2 % 2) * HALF, HALF), :], a_bufs[c].at[mine, pl.ds(0, MATS)]),
                (hf_rows.at[:, pl.ds(k2, 1)], a_bufs[c].at[mine, pl.ds(MATS, 1)]),
            )
        b, r0, rows = PIECES[c]
        columns = pl.ds(pl.multiple_of(k2 * COLS + (b % NCB) * BLK, BLK), BLK)
        return ((weights[b // NCB].at[:, pl.ds(r0, rows), columns], a_bufs[c].at[mine]),)

    def a_start(c):
        for d in range(1, EP):
            k2, j2 = partner(d)
            for src, dst in a_pairs(c, k2):
                pltpu.make_async_remote_copy(
                    src_ref=src, dst_ref=dst, send_sem=a_send.at[c], recv_sem=a_recv.at[c],
                    device_id=(k2, j2), device_id_type=MESH,
                ).start()
        for src, dst in a_pairs(c, k):
            pltpu.make_async_copy(src, dst, a_recv.at[c]).start()

    def b_start(c):
        a, b, land = a_bufs[c], b_bufs[c], l_bufs[c]

        @pl.loop(0, OWNERS)
        def _(s):
            b[s] = a[source[s]]

        @pl.loop(1, OWNERS)
        def _(o):
            s = owner(o)
            pltpu.make_async_remote_copy(
                src_ref=b.at[s], dst_ref=land.at[j], send_sem=b_send.at[c], recv_sem=b_recv.at[c],
                device_id=(k, s), device_id_type=MESH,
            ).start()

        pltpu.make_async_copy(b.at[j], land.at[j], b_recv.at[c]).start()

    for c in ORDER[:AUX_AT]:
        a_start(c)

    hf_copy.wait()

    @pl.loop(0, LOCAL)
    def _(e):
        factor = (ADAPTER_SCALE * active[e]).astype(jnp.float32)
        for k2 in range(EP):
            hf_wide[k2] = jnp.zeros((HALF, BLK), jnp.float32)
        for p in range(MATS):
            rows = hf_in[e, p].astype(jnp.float32) * factor
            for k2 in range(EP):
                for cb in range(NCB):
                    at = k2 * COLS + cb * BLK
                    hf_wide[k2, pl.ds(2 * (p * NCB + cb), 2), :] = rows[:, at : at + BLK]
        hf_rows[e] = hf_wide[...].astype(jnp.bfloat16)

    for c in ORDER[AUX_AT:]:
        a_start(c)

    @pl.loop(0, OWNERS)
    def _(s):
        found = jnp.int32(0)
        for e in range(EXPERTS):
            found = jnp.where(slot[e] == s, e, found)
        source[s] = found

    crossed = source[j] // (2 * LOCAL) - h
    crossed = crossed * crossed

    def sibling_copy():
        return pltpu.make_async_remote_copy(
            src_ref=l_bufs[AUX].at[:, pl.ds(0, MATS)], dst_ref=sibling, send_sem=c_send, recv_sem=c_recv,
            device_id=(k + 1 - 2 * core, j), device_id_type=MESH,
        )

    def b_wait(c):
        pltpu.make_async_copy(l_bufs[c], l_bufs[c], b_recv.at[c]).wait()

    def factors():
        b_wait(AUX)
        sibling_copy().start()
        packed = l_bufs[AUX][:, MATS].reshape(OWNERS * HALF, BLK)
        row = lax.broadcasted_iota(jnp.int32, (RANK, OWNERS * HALF), 0)
        col = lax.broadcasted_iota(jnp.int32, (RANK, OWNERS * HALF), 1)
        row = (row + core * HALF) % RANK
        holder = row // 2
        holder = holder + crossed * (4 - 8 * ((holder // 4) % 2))
        first = holder * HALF + row % 2
        for p in range(MATS):
            for cb in range(NCB):
                pick = jnp.where(col == first + 2 * (p * NCB + cb), 1.0, 0.0).astype(jnp.bfloat16)
                hf_all[p * NCB + cb] = jnp.dot(pick, packed, preferred_element_type=jnp.float32).astype(jnp.bfloat16)

    lanes = lax.broadcasted_iota(jnp.int32, (1, BLK), 1)

    def compute(b):
        pieces = [c for c in range(AUX) if PIECES[c][0] == b]
        for c in pieces:
            b_wait(c)
        aux, p = l_bufs[AUX], b // NCB

        def one(i, scales):
            held = i + crossed * (4 - 8 * ((i // 4) % 2))
            delta = lax.dot_general(
                jnp.concatenate([aux[held, p], sibling[held, p]], axis=0),
                hf_all[b],
                (((0,), (0,)), ((), ())),
                preferred_element_type=jnp.float32,
            )
            raw = [l_bufs[c][held].astype(jnp.float32) for c in pieces]
            merged = (raw[0] if len(raw) == 1 else jnp.concatenate(raw, axis=0)) + delta
            most = jnp.max(jnp.max(jnp.abs(merged), axis=0, keepdims=True), axis=1, keepdims=True)
            scale = (most + 1e-6).astype(jnp.bfloat16).astype(jnp.float32)
            out[b, i] = (merged * (1.0 / scale)).astype(jnp.bfloat16)
            return jnp.where(lanes == i, scale, scales)

        scales = lax.fori_loop(0, OWNERS, one, jnp.zeros((1, BLK), jnp.float32), unroll=4)
        scales_out[p, pl.ds(b % NCB, 1), :] = scales

    todo = [(ORDER.index(AUX), "factors")]
    todo += [(max(ORDER.index(c) for c in range(AUX) if PIECES[c][0] == b), b) for b in range(BLOCKS)]

    def work(until):
        while todo and todo[0][0] <= until:
            task = todo.pop(0)[1]
            if task == "factors":
                factors()
                continue
            if task == 0:
                sibling_copy().wait()
            compute(task)

    for at, c in enumerate(ORDER):
        pltpu.make_async_copy(a_bufs[c], a_bufs[c], a_recv.at[c]).wait()
        b_start(c)
        work(at - LAG)
    work(len(ORDER))

    for c in range(n):
        given = a_bufs[c].at[pl.ds(0, EXPERTS - LOCAL)]
        pltpu.make_async_copy(given, given, a_send.at[c]).wait()
        given = b_bufs[c].at[pl.ds(0, OWNERS - 1)]
        pltpu.make_async_copy(given, given, b_send.at[c]).wait()


def store(blocks, scales, out, scales_out, sem):
    copies = [
        pltpu.make_async_copy(
            blocks.at[b], out.at[b // NCB, :, :, pl.ds((b % NCB) * BLK, BLK)], sem.at[b]
        )
        for b in range(BLOCKS)
    ]
    for copy in copies:
        copy.start()
    for p in range(MATS):
        scales_out[p] = scales[p, :NCB, :OWNERS].astype(jnp.bfloat16)
    for copy in copies:
        copy.wait()


def on_device(
    gate_weight, up_weight, down_weight, model_factors, hidden_factors, active, expert_rollout_slot
):
    shapes = [(OWNERS, rows, BLK) for _, _, rows in PIECES] + [(OWNERS, MATS + 1, HALF, BLK)]
    bufs = [pltpu.VMEM(shape, jnp.bfloat16) for shape in shapes]
    smem, vmem, anywhere = (pl.BlockSpec(memory_space=s) for s in (pltpu.SMEM, pltpu.VMEM, pl.ANY))
    sems = pltpu.SemaphoreType.DMA
    n = len(bufs)

    blocks, scales = pl.pallas_call(
        kernel,
        out_shape=(
            pltpu.VMEM((BLOCKS, OWNERS, BLK, BLK), jnp.bfloat16),
            pltpu.VMEM((MATS, 8, BLK), jnp.float32),
        ),
        in_specs=[smem, smem] + [anywhere] * 5,
        out_specs=(vmem, vmem),
        scratch_shapes=bufs * 3 + [
            pltpu.VMEM((LOCAL, MATS, 2, EP * COLS), jnp.bfloat16),
            pltpu.VMEM((EP, HALF, BLK), jnp.float32),
            pltpu.VMEM((LOCAL, EP, HALF, BLK), jnp.bfloat16),
            pltpu.VMEM((OWNERS, MATS, HALF, BLK), jnp.bfloat16),
            pltpu.VMEM((BLOCKS, RANK, BLK), jnp.bfloat16),
            pltpu.SMEM((EXPERTS,), jnp.int32),
            sems((n,)), sems((n,)), sems((n,)), sems((n,)), sems, sems, sems,
        ],
        compiler_params=pltpu.CompilerParams(
            collective_id=0, has_side_effects=True, vmem_limit_bytes=46 * 1024 * 1024
        ),
    )(active, expert_rollout_slot, gate_weight, up_weight, down_weight, model_factors, hidden_factors)

    quantized, block_scales = pl.pallas_call(
        store,
        out_shape=(
            jax.ShapeDtypeStruct((MATS, OWNERS, BLK, COLS), jnp.bfloat16),
            jax.ShapeDtypeStruct((MATS, NCB, OWNERS), jnp.bfloat16),
        ),
        in_specs=[anywhere, vmem],
        out_specs=(anywhere, vmem),
        scratch_shapes=[sems((BLOCKS,))],
        compiler_params=pltpu.CompilerParams(vmem_limit_bytes=4 * 1024 * 1024),
    )(blocks, scales)
    return quantized.reshape(1, MATS, OWNERS * BLK, COLS), block_scales.transpose(0, 2, 1)[None]


def solution(mesh):
    placed = (
        P("ep", "fsdp", None),
        P("ep", "fsdp", None),
        P("ep", "fsdp", None),
        P("ep", None, None, "fsdp"),
        P("ep", None, "fsdp", None),
        P("ep"),
        P(),
    )
    return jax.shard_map(
        on_device,
        mesh=mesh,
        in_specs=placed,
        out_specs=(P("fsdp", None, None, "ep"), P("fsdp", None, None, "ep")),
        check_vma=False,
    )
```

time: 180 us -> 145 us (0.81)
  Pallas kernels: 164 us -> 144 us
  local copies, waits for them, and re-layouts: 10.9 us -> 0 us
  other arithmetic: 3.04 us -> 0 us
    pallas_call x1 -> x2, Pallas kernels: 164 us -> 144 us  [the longest x1 140 us: on_device(): pl.pallas_call(kernel, out_shape=(pltpu.VMEM((BLOCKS, OWNERS, BLK, BLK),...]
    unnamed x1 -> x0, local copies, waits for them, and re-layouts: 8.36 us -> none
where the time goes in v2:
time: 145 us
  Pallas kernels  144 us (99%)
    pallas_call x1, Pallas kernels, on_device(): pl.pallas_call(kernel, out_shape=(pltpu.VMEM((BLOCKS, OWNERS, BLK, BLK),...  140 us
    pallas_call x1, Pallas kernels, on_device(): pl.pallas_call(store, out_shape=(jax.ShapeDtypeStruct((MATS, OWNERS, BLK,...  4.27 us

profile of v2, /device:TPU:3, one launch (start us, length us, event | category | flops | bytes accessed | tf_op | source)
XLA Modules:
  0.0 144.6 jit_solution(12356202791541873467)
XLA Ops:
  0.6 139.7 %shard_map.86 = (bf16[9,32,128,128]{3,2,1,0:T(8,128)(2,1)S(1)}, f32[3,8,128]{2,1,0:T(8,128)S(1)}) custom-call(s32[8]{0:T(128)} %active.1, s32[32]{0:T(128)} %slot.1, bf16[8,128,1536]{2,1,0:T(8,128)(2,1)} %gate.1, bf16[8,128,1536]{2,1,0:T(8,128)(2,1)} %up.1, bf16[8,128,1536]{2,1,0:T(8,128)(2,1)} %down.1, bf16[8,3,64,128]{3,2,1,0:T(8,128)(2,1)} %mf.1, ...), custom_call_target="tpu_custom_call" | custom-call | tf_op jit(solution)/shard_map/pallas_call | solution.py:236
  140.3 4.3 %shard_map.87 = (bf16[3,32,128,384]{3,2,1,0:T(8,128)(2,1)}, bf16[3,3,32]{2,1,0:T(4,128)(2,1)}) custom-call(bf16[9,32,128,128]{3,2,1,0:T(8,128)(2,1)S(1)} %get-tuple-element.6.blocks, f32[3,8,128]{2,1,0:T(8,128)S(1)} %get-tuple-element.7.scales), custom_call_target="tpu_custom_call" | custom-call | tf_op jit(solution)/shard_map/pallas_call | solution.py:258

commit v3 on v2

--- a/solution.py
+++ b/solution.py
@@ -25,15 +25,40 @@
 AUX_AT = 2
 ORDER = tuple(range(AUX_AT)) + (AUX,) + tuple(range(AUX_AT, AUX))
 LAG = 2
+LAST = BLOCKS - 1
+LAST_PIECES = tuple(c for c in range(AUX) if PIECES[c][0] == LAST)
+STORE = 8
 STEP = 13
 MESH = pl.DeviceIdType.MESH
 
 
-def kernel(active, slot, gate, up, down, mf, hf, out, scales_out, *scratch):
+def crossing(home):
+    away = home // (2 * LOCAL) - lax.axis_index("ep") // 2
+    return away * away
+
+
+def merge(i, crossed, aux, sibling, factors, pieces, p):
+    held = i + crossed * (4 - 8 * ((i // 4) % 2))
+    delta = lax.dot_general(
+        jnp.concatenate([aux[held, p], sibling[held, p]], axis=0),
+        factors,
+        (((0,), (0,)), ((), ())),
+        preferred_element_type=jnp.float32,
+    )
+    raw = [piece[held].astype(jnp.float32) for piece in pieces]
+    merged = (raw[0] if len(raw) == 1 else jnp.concatenate(raw, axis=0)) + delta
+    most = jnp.max(jnp.max(jnp.abs(merged), axis=0, keepdims=True), axis=1, keepdims=True)
+    scale = (most + 1e-6).astype(jnp.bfloat16).astype(jnp.float32)
+    return (merged * (1.0 / scale)).astype(jnp.bfloat16), scale
+
+
+def kernel(active, slot, gate, up, down, mf, hf, out, scales_out, hf_all, sibling, *refs):
     n = AUX + 1
-    a_bufs, b_bufs, l_bufs = scratch[:n], scratch[n : 2 * n], scratch[2 * n : 3 * n]
-    (hf_in, hf_wide, hf_rows, sibling, hf_all, source,
-     a_send, a_recv, b_send, b_recv, c_send, c_recv, in_sem) = scratch[3 * n :]
+    kept, refs = refs[: len(LAST_PIECES) + 1], refs[len(LAST_PIECES) + 1 :]
+    first = n - len(kept)
+    a_bufs, b_bufs, l_bufs = refs[:n], refs[n : 2 * n], refs[2 * n : 2 * n + first] + kept
+    (hf_in, hf_wide, hf_rows, source,
+     a_send, a_recv, b_send, b_recv, c_send, c_recv, in_sem) = refs[2 * n + first :]
     weights = (gate, up, down)
 
     k, j = lax.axis_index("ep"), lax.axis_index("fsdp")
@@ -130,8 +155,7 @@
             found = jnp.where(slot[e] == s, e, found)
         source[s] = found
 
-    crossed = source[j] // (2 * LOCAL) - h
-    crossed = crossed * crossed
+    crossed = crossing(source[j])
 
     def sibling_copy():
         return pltpu.make_async_remote_copy(
@@ -163,21 +187,14 @@
         pieces = [c for c in range(AUX) if PIECES[c][0] == b]
         for c in pieces:
             b_wait(c)
-        aux, p = l_bufs[AUX], b // NCB
+        if b == LAST:
+            return
+        p, columns = b // NCB, slice((b % NCB) * BLK, (b % NCB + 1) * BLK)
 
         def one(i, scales):
-            held = i + crossed * (4 - 8 * ((i // 4) % 2))
-            delta = lax.dot_general(
-                jnp.concatenate([aux[held, p], sibling[held, p]], axis=0),
-                hf_all[b],
-                (((0,), (0,)), ((), ())),
-                preferred_element_type=jnp.float32,
+            out[p, i, :, columns], scale = merge(
+                i, crossed, l_bufs[AUX], sibling, hf_all[b], [l_bufs[c] for c in pieces], p
             )
-            raw = [l_bufs[c][held].astype(jnp.float32) for c in pieces]
-            merged = (raw[0] if len(raw) == 1 else jnp.concatenate(raw, axis=0)) + delta
-            most = jnp.max(jnp.max(jnp.abs(merged), axis=0, keepdims=True), axis=1, keepdims=True)
-            scale = (most + 1e-6).astype(jnp.bfloat16).astype(jnp.float32)
-            out[b, i] = (merged * (1.0 / scale)).astype(jnp.bfloat16)
             return jnp.where(lanes == i, scale, scales)
 
         scales = lax.fori_loop(0, OWNERS, one, jnp.zeros((1, BLK), jnp.float32), unroll=4)
@@ -209,17 +226,43 @@
         pltpu.make_async_copy(given, given, b_send.at[c]).wait()
 
 
-def store(blocks, scales, out, scales_out, sem):
-    copies = [
-        pltpu.make_async_copy(
-            blocks.at[b], out.at[b // NCB, :, :, pl.ds((b % NCB) * BLK, BLK)], sem.at[b]
-        )
-        for b in range(BLOCKS)
-    ]
-    for copy in copies:
-        copy.start()
-    for p in range(MATS):
-        scales_out[p] = scales[p, :NCB, :OWNERS].astype(jnp.bfloat16)
+def store(slot, blocks, scales, hf_all, sibling, *refs):
+    pieces, aux = refs[: len(LAST_PIECES)], refs[len(LAST_PIECES)]
+    out, scales_out, last, sem = refs[len(LAST_PIECES) + 1 :]
+    p, cb = LAST // NCB, LAST % NCB
+    copies = []
+
+    def begin(src, dst):
+        copies.append(pltpu.make_async_copy(src, dst, sem.at[len(copies)]))
+        copies[-1].start()
+
+    for q in range(MATS):
+        for i in range(0, OWNERS, STORE):
+            rows = pl.ds(i, STORE)
+            if q == p:
+                begin(blocks.at[q, rows, :, pl.ds(0, cb * BLK)], out.at[q, rows, :, pl.ds(0, cb * BLK)])
+            else:
+                begin(blocks.at[q, rows], out.at[q, rows])
+
+    j = lax.axis_index("fsdp")
+    home = jnp.int32(0)
+    for e in range(EXPERTS):
+        home = jnp.where(slot[e] == j, e, home)
+    crossed = crossing(home)
+    lanes = lax.broadcasted_iota(jnp.int32, (1, BLK), 1)
+
+    def one(i, scales_now):
+        last[i], scale = merge(i, crossed, aux, sibling, hf_all[LAST], pieces, p)
+        return jnp.where(lanes == i, scale, scales_now)
+
+    final = jnp.zeros((1, BLK), jnp.float32)
+    for i in range(0, OWNERS, STORE):
+        final = lax.fori_loop(i, i + STORE, one, final, unroll=4)
+        rows = pl.ds(i, STORE)
+        begin(last.at[rows], out.at[p, rows, :, pl.ds(cb * BLK, BLK)])
+    for q in range(MATS):
+        scales_out[q] = scales[q, :NCB, :OWNERS].astype(jnp.bfloat16)
+    scales_out[p, cb : cb + 1, :] = final[:, :OWNERS].astype(jnp.bfloat16)
     for copy in copies:
         copy.wait()
 
@@ -233,25 +276,27 @@
     sems = pltpu.SemaphoreType.DMA
     n = len(bufs)
 
-    blocks, scales = pl.pallas_call(
+    kept = len(LAST_PIECES) + 1
+    made = pl.pallas_call(
         kernel,
         out_shape=(
-            pltpu.VMEM((BLOCKS, OWNERS, BLK, BLK), jnp.bfloat16),
+            pltpu.VMEM((MATS, OWNERS, BLK, COLS), jnp.bfloat16),
             pltpu.VMEM((MATS, 8, BLK), jnp.float32),
+            pltpu.VMEM((BLOCKS, RANK, BLK), jnp.bfloat16),
+            pltpu.VMEM((OWNERS, MATS, HALF, BLK), jnp.bfloat16),
+            *bufs[n - kept :],
         ),
         in_specs=[smem, smem] + [anywhere] * 5,
-        out_specs=(vmem, vmem),
-        scratch_shapes=bufs * 3 + [
+        out_specs=(vmem,) * (4 + kept),
+        scratch_shapes=bufs * 2 + bufs[: n - kept] + [
             pltpu.VMEM((LOCAL, MATS, 2, EP * COLS), jnp.bfloat16),
             pltpu.VMEM((EP, HALF, BLK), jnp.float32),
             pltpu.VMEM((LOCAL, EP, HALF, BLK), jnp.bfloat16),
-            pltpu.VMEM((OWNERS, MATS, HALF, BLK), jnp.bfloat16),
-            pltpu.VMEM((BLOCKS, RANK, BLK), jnp.bfloat16),
             pltpu.SMEM((EXPERTS,), jnp.int32),
             sems((n,)), sems((n,)), sems((n,)), sems((n,)), sems, sems, sems,
         ],
         compiler_params=pltpu.CompilerParams(
-            collective_id=0, has_side_effects=True, vmem_limit_bytes=46 * 1024 * 1024
+            collective_id=0, has_side_effects=True, vmem_limit_bytes=50 * 1024 * 1024
         ),
     )(active, expert_rollout_slot, gate_weight, up_weight, down_weight, model_factors, hidden_factors)
 
@@ -261,11 +306,11 @@
             jax.ShapeDtypeStruct((MATS, OWNERS, BLK, COLS), jnp.bfloat16),
             jax.ShapeDtypeStruct((MATS, NCB, OWNERS), jnp.bfloat16),
         ),
-        in_specs=[anywhere, vmem],
+        in_specs=[smem, anywhere] + [vmem] * (3 + kept),
         out_specs=(anywhere, vmem),
-        scratch_shapes=[sems((BLOCKS,))],
-        compiler_params=pltpu.CompilerParams(vmem_limit_bytes=4 * 1024 * 1024),
-    )(blocks, scales)
+        scratch_shapes=[pltpu.VMEM((OWNERS, BLK, BLK), jnp.bfloat16), sems(((MATS + 1) * OWNERS // STORE,))],
+        compiler_params=pltpu.CompilerParams(vmem_limit_bytes=8 * 1024 * 1024),
+    )(expert_rollout_slot, *made)
     return quantized.reshape(1, MATS, OWNERS * BLK, COLS), block_scales.transpose(0, 2, 1)[None]
 
 

time: 145 us -> 143 us (0.986)
  Pallas kernels: 144 us -> 142 us
    pallas_call x1, Pallas kernels: 140 us -> 137 us  [on_device(): pl.pallas_call(kernel, out_shape=(pltpu.VMEM((MATS, OWNERS, BLK, COLS), j...]
where the time goes in v3:
time: 143 us; the launch traced here: 142 us
  Pallas kernels  142 us (99%)
    pallas_call x1, Pallas kernels, on_device(): pl.pallas_call(kernel, out_shape=(pltpu.VMEM((MATS, OWNERS, BLK, COLS), j...  137 us
    pallas_call x1, Pallas kernels, on_device(): pl.pallas_call(store, out_shape=(jax.ShapeDtypeStruct((MATS, OWNERS, BLK,...  4.85 us

profile of v3, /device:TPU:3, one launch (start us, length us, event | category | flops | bytes accessed | tf_op | source)
XLA Modules:
  0.0 142.4 jit_solution(12715392090820905687)
XLA Ops:
  0.6 0.0 copy-start
  0.6 136.9 %shard_map.86 = (bf16[3,32,128,384]{3,2,1,0:T(8,128)(2,1)S(1)}, f32[3,8,128]{2,1,0:T(8,128)S(1)}, bf16[9,64,128]{2,1,0:T(8,128)(2,1)S(1)}, bf16[32,3,32,128]{3,2...) custom-call(s32[8]{0:T(128)} %active.1, s32[32]{0:T(128)} %slot.3, ...), custom_call_target="tpu_custom_call" | custom-call | tf_op jit(solution)/shard_map/pallas_call | solution.py:280
  137.6 0.0 copy-done
  137.6 4.9 %shard_map.87 = (bf16[3,32,128,384]{3,2,1,0:T(8,128)(2,1)}, bf16[3,3,32]{2,1,0:T(4,128)(2,1)}) custom-call(s32[32]{0:T(128)S(1)} %copy-done, bf16[3,32,128,384]{3,2,1,0:T(8,128)(2,1)S(1)} %get-tuple-element.11.blocks, f32[3,8,128]{2,1,0:T(8,128)S(1)} %get-tuple-element.12.scales, bf16[9,64,128]{2,1,0:T(8,128)(2,1)S(1)} %get-tuple-element.13.hf_all, ...), custom_call_target="tpu_custom_call" | custom-call | tf_op jit(solution)/shard_map/pallas_call | solution.py:303
Async XLA Ops:
  0.6 137.0 %copy-start = (s32[32]{0:T(128)S(1)}, s32[32]{0:T(128)}, u32[]{:S(2)}) copy-start(s32[32]{0:T(128)} %slot.3) | copy-start | bytes 388

commit v4 on v3

--- a/solution.py
+++ b/solution.py
@@ -52,12 +52,12 @@
     return (merged * (1.0 / scale)).astype(jnp.bfloat16), scale
 
 
-def kernel(active, slot, gate, up, down, mf, hf, out, scales_out, hf_all, sibling, *refs):
+def kernel(active_in, slot_in, gate, up, down, mf, hf, out, scales_out, hf_all, sibling, *refs):
     n = AUX + 1
     kept, refs = refs[: len(LAST_PIECES) + 1], refs[len(LAST_PIECES) + 1 :]
     first = n - len(kept)
     a_bufs, b_bufs, l_bufs = refs[:n], refs[n : 2 * n], refs[2 * n : 2 * n + first] + kept
-    (hf_in, hf_wide, hf_rows, source,
+    (hf_in, hf_wide, hf_rows, active, slot, source,
      a_send, a_recv, b_send, b_recv, c_send, c_recv, in_sem) = refs[2 * n + first :]
     weights = (gate, up, down)
 
@@ -79,12 +79,16 @@
     for d in range(1, EP):
         pl.semaphore_signal(barrier, inc=1, device_id=partner(d), device_id_type=MESH)
 
-    @pl.loop(1, OWNERS)
+    @pl.loop(1, OWNERS, unroll=True)
     def _(o):
         pl.semaphore_signal(barrier, inc=1, device_id=(k, owner(o)), device_id_type=MESH)
 
-    hf_copy = pltpu.make_async_copy(hf, hf_in, in_sem)
-    hf_copy.start()
+    fetches = [
+        pltpu.make_async_copy(src, dst, in_sem.at[q])
+        for q, (src, dst) in enumerate(((hf, hf_in), (active_in, active), (slot_in, slot)))
+    ]
+    for fetch in fetches:
+        fetch.start()
     pl.semaphore_wait(barrier, EP - 1 + OWNERS - 1)
 
     mine = pl.ds(k * LOCAL, LOCAL)
@@ -130,7 +134,8 @@
     for c in ORDER[:AUX_AT]:
         a_start(c)
 
-    hf_copy.wait()
+    for fetch in fetches:
+        fetch.wait()
 
     @pl.loop(0, LOCAL)
     def _(e):
@@ -217,20 +222,28 @@
         pltpu.make_async_copy(a_bufs[c], a_bufs[c], a_recv.at[c]).wait()
         b_start(c)
         work(at - LAG)
-    work(len(ORDER))
-
-    for c in range(n):
+
+    def b_sent(c):
+        given = b_bufs[c].at[pl.ds(0, OWNERS - 1)]
+        pltpu.make_async_copy(given, given, b_send.at[c]).wait()
+
+    for c in ORDER:
         given = a_bufs[c].at[pl.ds(0, EXPERTS - LOCAL)]
         pltpu.make_async_copy(given, given, a_send.at[c]).wait()
-        given = b_bufs[c].at[pl.ds(0, OWNERS - 1)]
-        pltpu.make_async_copy(given, given, b_send.at[c]).wait()
-
-
-def store(slot, blocks, scales, hf_all, sibling, *refs):
+        if c not in LAST_PIECES:
+            b_sent(c)
+    work(len(ORDER))
+    for c in LAST_PIECES:
+        b_sent(c)
+
+
+def store(slot_in, blocks, scales, hf_all, sibling, *refs):
     pieces, aux = refs[: len(LAST_PIECES)], refs[len(LAST_PIECES)]
-    out, scales_out, last, sem = refs[len(LAST_PIECES) + 1 :]
+    out, scales_out, slot, last, slot_sem, sem = refs[len(LAST_PIECES) + 1 :]
     p, cb = LAST // NCB, LAST % NCB
     copies = []
+    fetch = pltpu.make_async_copy(slot_in, slot, slot_sem)
+    fetch.start()
 
     def begin(src, dst):
         copies.append(pltpu.make_async_copy(src, dst, sem.at[len(copies)]))
@@ -244,6 +257,7 @@
             else:
                 begin(blocks.at[q, rows], out.at[q, rows])
 
+    fetch.wait()
     j = lax.axis_index("fsdp")
     home = jnp.int32(0)
     for e in range(EXPERTS):
@@ -272,7 +286,7 @@
 ):
     shapes = [(OWNERS, rows, BLK) for _, _, rows in PIECES] + [(OWNERS, MATS + 1, HALF, BLK)]
     bufs = [pltpu.VMEM(shape, jnp.bfloat16) for shape in shapes]
-    smem, vmem, anywhere = (pl.BlockSpec(memory_space=s) for s in (pltpu.SMEM, pltpu.VMEM, pl.ANY))
+    vmem, anywhere = (pl.BlockSpec(memory_space=s) for s in (pltpu.VMEM, pl.ANY))
     sems = pltpu.SemaphoreType.DMA
     n = len(bufs)
 
@@ -286,14 +300,16 @@
             pltpu.VMEM((OWNERS, MATS, HALF, BLK), jnp.bfloat16),
             *bufs[n - kept :],
         ),
-        in_specs=[smem, smem] + [anywhere] * 5,
+        in_specs=[anywhere] * 7,
         out_specs=(vmem,) * (4 + kept),
         scratch_shapes=bufs * 2 + bufs[: n - kept] + [
             pltpu.VMEM((LOCAL, MATS, 2, EP * COLS), jnp.bfloat16),
             pltpu.VMEM((EP, HALF, BLK), jnp.float32),
             pltpu.VMEM((LOCAL, EP, HALF, BLK), jnp.bfloat16),
+            pltpu.SMEM((LOCAL,), jnp.int32),
             pltpu.SMEM((EXPERTS,), jnp.int32),
-            sems((n,)), sems((n,)), sems((n,)), sems((n,)), sems, sems, sems,
+            pltpu.SMEM((EXPERTS,), jnp.int32),
+            sems((n,)), sems((n,)), sems((n,)), sems((n,)), sems, sems, sems((3,)),
         ],
         compiler_params=pltpu.CompilerParams(
             collective_id=0, has_side_effects=True, vmem_limit_bytes=50 * 1024 * 1024
@@ -306,9 +322,9 @@
             jax.ShapeDtypeStruct((MATS, OWNERS, BLK, COLS), jnp.bfloat16),
             jax.ShapeDtypeStruct((MATS, NCB, OWNERS), jnp.bfloat16),
         ),
-        in_specs=[smem, anywhere] + [vmem] * (3 + kept),
+        in_specs=[anywhere, anywhere] + [vmem] * (3 + kept),
         out_specs=(anywhere, vmem),
-        scratch_shapes=[pltpu.VMEM((OWNERS, BLK, BLK), jnp.bfloat16), sems(((MATS + 1) * OWNERS // STORE,))],
+        scratch_shapes=[pltpu.SMEM((EXPERTS,), jnp.int32), pltpu.VMEM((OWNERS, BLK, BLK), jnp.bfloat16), sems, sems(((MATS + 1) * OWNERS // STORE,))],
         compiler_params=pltpu.CompilerParams(vmem_limit_bytes=8 * 1024 * 1024),
     )(expert_rollout_slot, *made)
     return quantized.reshape(1, MATS, OWNERS * BLK, COLS), block_scales.transpose(0, 2, 1)[None]

time: 143 us -> 141 us (0.986)
  Pallas kernels: 142 us -> 140 us
    pallas_call x1, Pallas kernels: 137 us -> 135 us  [on_device(): pl.pallas_call(kernel, out_shape=(pltpu.VMEM((MATS, OWNERS, BLK, COLS), j...]
where the time goes in v4:
time: 141 us
  Pallas kernels  140 us (99%)
    pallas_call x1, Pallas kernels, on_device(): pl.pallas_call(kernel, out_shape=(pltpu.VMEM((MATS, OWNERS, BLK, COLS), j...  135 us
    pallas_call x1, Pallas kernels, on_device(): pl.pallas_call(store, out_shape=(jax.ShapeDtypeStruct((MATS, OWNERS, BLK,...  4.74 us

profile of v4, /device:TPU:3, one launch (start us, length us, event | category | flops | bytes accessed | tf_op | source)
XLA Modules:
  0.0 140.8 jit_solution(6782334808123917355)
XLA Ops:
  0.6 0.0 copy-start
  0.6 135.4 %shard_map.86 = (bf16[3,32,128,384]{3,2,1,0:T(8,128)(2,1)S(1)}, f32[3,8,128]{2,1,0:T(8,128)S(1)}, bf16[9,64,128]{2,1,0:T(8,128)(2,1)S(1)}, bf16[32,3,32,128]{3,2...) custom-call(s32[8]{0:T(128)} %active_in.1, ...), custom_call_target="tpu_custom_call" | custom-call | tf_op jit(solution)/shard_map/pallas_call | solution.py:294
  136.0 0.0 copy-done
  136.0 4.7 %shard_map.87 = (bf16[3,32,128,384]{3,2,1,0:T(8,128)(2,1)}, bf16[3,3,32]{2,1,0:T(4,128)(2,1)}) custom-call(s32[32]{0:T(128)S(1)} %copy-done, bf16[3,32,128,384]{3,2,1,0:T(8,128)(2,1)S(1)} %get-tuple-element.11.blocks, f32[3,8,128]{2,1,0:T(8,128)S(1)} %get-tuple-element.12.scales, bf16[9,64,128]{2,1,0:T(8,128)(2,1)S(1)} %get-tuple-element.13.hf_all, ...), custom_call_target="tpu_custom_call" | custom-call | tf_op jit(solution)/shard_map/pallas_call | solution.py:319
Async XLA Ops:
  0.6 135.4 %copy-start = (s32[32]{0:T(128)S(1)}, s32[32]{0:T(128)}, u32[]{:S(2)}) copy-start(s32[32]{0:T(128)} %slot_in.3) | copy-start | bytes 388

commit v5 on v4

--- a/solution.py
+++ b/solution.py
@@ -17,14 +17,16 @@
 COLS = 384
 NCB = COLS // BLK
 BLOCKS = MATS * NCB
-ROWS = ((64, 64),) + ((128,),) * 7 + ((64, 64),)
+ROWS = ((48, 48, 32),) * 9
 PIECES = tuple(
     (b, sum(cut[:i]), rows) for b, cut in enumerate(ROWS) for i, rows in enumerate(cut)
 )
 AUX = len(PIECES)
+FACTORS = (AUX, AUX + 1)
+ALL = AUX + len(FACTORS)
 AUX_AT = 2
-ORDER = tuple(range(AUX_AT)) + (AUX,) + tuple(range(AUX_AT, AUX))
-LAG = 2
+ORDER = tuple(range(AUX_AT)) + FACTORS + tuple(range(AUX_AT, AUX))
+LAG = 4
 LAST = BLOCKS - 1
 LAST_PIECES = tuple(c for c in range(AUX) if PIECES[c][0] == LAST)
 STORE = 8
@@ -40,7 +42,7 @@
 def merge(i, crossed, aux, sibling, factors, pieces, p):
     held = i + crossed * (4 - 8 * ((i // 4) % 2))
     delta = lax.dot_general(
-        jnp.concatenate([aux[held, p], sibling[held, p]], axis=0),
+        jnp.concatenate([aux[p // 2][held, p % 2], sibling[held, p]], axis=0),
         factors,
         (((0,), (0,)), ((), ())),
         preferred_element_type=jnp.float32,
@@ -53,8 +55,8 @@
 
 
 def kernel(active_in, slot_in, gate, up, down, mf, hf, out, scales_out, hf_all, sibling, *refs):
-    n = AUX + 1
-    kept, refs = refs[: len(LAST_PIECES) + 1], refs[len(LAST_PIECES) + 1 :]
+    n = ALL
+    kept, refs = refs[: len(LAST_PIECES) + 2], refs[len(LAST_PIECES) + 2 :]
     first = n - len(kept)
     a_bufs, b_bufs, l_bufs = refs[:n], refs[n : 2 * n], refs[2 * n : 2 * n + first] + kept
     (hf_in, hf_wide, hf_rows, active, slot, source,
@@ -94,10 +96,13 @@
     mine = pl.ds(k * LOCAL, LOCAL)
 
     def a_pairs(c, k2):
+        half = pl.ds((k2 % 2) * HALF, HALF)
         if c == AUX:
+            return ((mf.at[:, pl.ds(0, 2), half, :], a_bufs[c].at[mine]),)
+        if c == AUX + 1:
             return (
-                (mf.at[:, :, pl.ds((k2 % 2) * HALF, HALF), :], a_bufs[c].at[mine, pl.ds(0, MATS)]),
-                (hf_rows.at[:, pl.ds(k2, 1)], a_bufs[c].at[mine, pl.ds(MATS, 1)]),
+                (mf.at[:, pl.ds(2, 1), half, :], a_bufs[c].at[mine, pl.ds(0, 1)]),
+                (hf_rows.at[:, pl.ds(k2, 1)], a_bufs[c].at[mine, pl.ds(1, 1)]),
             )
         b, r0, rows = PIECES[c]
         columns = pl.ds(pl.multiple_of(k2 * COLS + (b % NCB) * BLK, BLK), BLK)
@@ -162,19 +167,24 @@
 
     crossed = crossing(source[j])
 
-    def sibling_copy():
-        return pltpu.make_async_remote_copy(
-            src_ref=l_bufs[AUX].at[:, pl.ds(0, MATS)], dst_ref=sibling, send_sem=c_send, recv_sem=c_recv,
-            device_id=(k + 1 - 2 * core, j), device_id_type=MESH,
-        )
+    def sibling_copies():
+        return [
+            pltpu.make_async_remote_copy(
+                src_ref=l_bufs[AUX + q].at[:, pl.ds(0, mats)], dst_ref=sibling.at[:, pl.ds(2 * q, mats)],
+                send_sem=c_send.at[q], recv_sem=c_recv.at[q],
+                device_id=(k + 1 - 2 * core, j), device_id_type=MESH,
+            )
+            for q, mats in ((0, 2), (1, 1))
+        ]
 
     def b_wait(c):
         pltpu.make_async_copy(l_bufs[c], l_bufs[c], b_recv.at[c]).wait()
 
     def factors():
-        b_wait(AUX)
-        sibling_copy().start()
-        packed = l_bufs[AUX][:, MATS].reshape(OWNERS * HALF, BLK)
+        for c, copy in zip(FACTORS, sibling_copies()):
+            b_wait(c)
+            copy.start()
+        packed = l_bufs[AUX + 1][:, 1].reshape(OWNERS * HALF, BLK)
         row = lax.broadcasted_iota(jnp.int32, (RANK, OWNERS * HALF), 0)
         col = lax.broadcasted_iota(jnp.int32, (RANK, OWNERS * HALF), 1)
         row = (row + core * HALF) % RANK
@@ -198,14 +208,14 @@
 
         def one(i, scales):
             out[p, i, :, columns], scale = merge(
-                i, crossed, l_bufs[AUX], sibling, hf_all[b], [l_bufs[c] for c in pieces], p
+                i, crossed, l_bufs[AUX:], sibling, hf_all[b], [l_bufs[c] for c in pieces], p
             )
             return jnp.where(lanes == i, scale, scales)
 
         scales = lax.fori_loop(0, OWNERS, one, jnp.zeros((1, BLK), jnp.float32), unroll=4)
         scales_out[p, pl.ds(b % NCB, 1), :] = scales
 
-    todo = [(ORDER.index(AUX), "factors")]
+    todo = [(max(ORDER.index(c) for c in FACTORS), "factors")]
     todo += [(max(ORDER.index(c) for c in range(AUX) if PIECES[c][0] == b), b) for b in range(BLOCKS)]
 
     def work(until):
@@ -215,7 +225,8 @@
                 factors()
                 continue
             if task == 0:
-                sibling_copy().wait()
+                for copy in sibling_copies():
+                    copy.wait()
             compute(task)
 
     for at, c in enumerate(ORDER):
@@ -238,8 +249,8 @@
 
 
 def store(slot_in, blocks, scales, hf_all, sibling, *refs):
-    pieces, aux = refs[: len(LAST_PIECES)], refs[len(LAST_PIECES)]
-    out, scales_out, slot, last, slot_sem, sem = refs[len(LAST_PIECES) + 1 :]
+    pieces, aux = refs[: len(LAST_PIECES)], refs[len(LAST_PIECES) : len(LAST_PIECES) + 2]
+    out, scales_out, slot, last, slot_sem, sem = refs[len(LAST_PIECES) + 2 :]
     p, cb = LAST // NCB, LAST % NCB
     copies = []
     fetch = pltpu.make_async_copy(slot_in, slot, slot_sem)
@@ -284,13 +295,13 @@
 def on_device(
     gate_weight, up_weight, down_weight, model_factors, hidden_factors, active, expert_rollout_slot
 ):
-    shapes = [(OWNERS, rows, BLK) for _, _, rows in PIECES] + [(OWNERS, MATS + 1, HALF, BLK)]
+    shapes = [(OWNERS, rows, BLK) for _, _, rows in PIECES] + [(OWNERS, 2, HALF, BLK)] * 2
     bufs = [pltpu.VMEM(shape, jnp.bfloat16) for shape in shapes]
     vmem, anywhere = (pl.BlockSpec(memory_space=s) for s in (pltpu.VMEM, pl.ANY))
     sems = pltpu.SemaphoreType.DMA
     n = len(bufs)
 
-    kept = len(LAST_PIECES) + 1
+    kept = len(LAST_PIECES) + 2
     made = pl.pallas_call(
         kernel,
         out_shape=(
@@ -309,7 +320,7 @@
             pltpu.SMEM((LOCAL,), jnp.int32),
             pltpu.SMEM((EXPERTS,), jnp.int32),
             pltpu.SMEM((EXPERTS,), jnp.int32),
-            sems((n,)), sems((n,)), sems((n,)), sems((n,)), sems, sems, sems((3,)),
+            sems((n,)), sems((n,)), sems((n,)), sems((n,)), sems((2,)), sems((2,)), sems((3,)),
         ],
         compiler_params=pltpu.CompilerParams(
             collective_id=0, has_side_effects=True, vmem_limit_bytes=50 * 1024 * 1024

time: 141 us -> 138 us (0.979); the launches traced: 141 us -> 136 us
  Pallas kernels: 140 us -> 135 us
    pallas_call x1, Pallas kernels: 135 us -> 131 us  [on_device(): pl.pallas_call(kernel, out_shape=(pltpu.VMEM((MATS, OWNERS, BLK, COLS), j...]
where the time goes in v5:
time: 138 us; the launch traced here: 136 us
  Pallas kernels  135 us (98%)
    pallas_call x1, Pallas kernels, on_device(): pl.pallas_call(kernel, out_shape=(pltpu.VMEM((MATS, OWNERS, BLK, COLS), j...  131 us
    pallas_call x1, Pallas kernels, on_device(): pl.pallas_call(store, out_shape=(jax.ShapeDtypeStruct((MATS, OWNERS, BLK,...  4.73 us

profile of v5, /device:TPU:3, one launch (start us, length us, event | category | flops | bytes accessed | tf_op | source)
XLA Modules:
  0.0 136.1 jit_solution(8420559811238257335)
XLA Ops:
  0.6 0.0 copy-start
  0.6 130.7 %shard_map.86 = (bf16[3,32,128,384]{3,2,1,0:T(8,128)(2,1)S(1)}, f32[3,8,128]{2,1,0:T(8,128)S(1)}, bf16[9,64,128]{2,1,0:T(8,128)(2,1)S(1)}, bf16[32,3,32,128]{3,2...) custom-call(s32[8]{0:T(128)} %active_in.1, ...), custom_call_target="tpu_custom_call" | custom-call | tf_op jit(solution)/shard_map/pallas_call | solution.py:305
  131.3 0.0 copy-done
  131.3 4.7 %shard_map.87 = (bf16[3,32,128,384]{3,2,1,0:T(8,128)(2,1)}, bf16[3,3,32]{2,1,0:T(4,128)(2,1)}) custom-call(s32[32]{0:T(128)S(1)} %copy-done, bf16[3,32,128,384]{3,2,1,0:T(8,128)(2,1)S(1)} %get-tuple-element.13.blocks, f32[3,8,128]{2,1,0:T(8,128)S(1)} %get-tuple-element.14.scales, bf16[9,64,128]{2,1,0:T(8,128)(2,1)S(1)} %get-tuple-element.15.hf_all, ...), custom_call_target="tpu_custom_call" | custom-call | tf_op jit(solution)/shard_map/pallas_call | solution.py:330
Async XLA Ops:
  0.6 130.7 %copy-start = (s32[32]{0:T(128)S(1)}, s32[32]{0:T(128)}, u32[]{:S(2)}) copy-start(s32[32]{0:T(128)} %slot_in.3) | copy-start | bytes 388

commit v6 on v5

--- a/solution.py
+++ b/solution.py
@@ -22,7 +22,7 @@
     (b, sum(cut[:i]), rows) for b, cut in enumerate(ROWS) for i, rows in enumerate(cut)
 )
 AUX = len(PIECES)
-FACTORS = (AUX, AUX + 1)
+FACTORS = tuple(range(AUX, AUX + MATS + 1))
 ALL = AUX + len(FACTORS)
 AUX_AT = 2
 ORDER = tuple(range(AUX_AT)) + FACTORS + tuple(range(AUX_AT, AUX))
@@ -42,7 +42,7 @@
 def merge(i, crossed, aux, sibling, factors, pieces, p):
     held = i + crossed * (4 - 8 * ((i // 4) % 2))
     delta = lax.dot_general(
-        jnp.concatenate([aux[p // 2][held, p % 2], sibling[held, p]], axis=0),
+        jnp.concatenate([aux[p][held, 0], sibling[held, p]], axis=0),
         factors,
         (((0,), (0,)), ((), ())),
         preferred_element_type=jnp.float32,
@@ -56,7 +56,7 @@
 
 def kernel(active_in, slot_in, gate, up, down, mf, hf, out, scales_out, hf_all, sibling, *refs):
     n = ALL
-    kept, refs = refs[: len(LAST_PIECES) + 2], refs[len(LAST_PIECES) + 2 :]
+    kept, refs = refs[: len(LAST_PIECES + FACTORS)], refs[len(LAST_PIECES + FACTORS) :]
     first = n - len(kept)
     a_bufs, b_bufs, l_bufs = refs[:n], refs[n : 2 * n], refs[2 * n : 2 * n + first] + kept
     (hf_in, hf_wide, hf_rows, active, slot, source,
@@ -74,8 +74,10 @@
         return k2, j + dh * dh * flip
 
     def owner(o):
-        o = (o * STEP) % OWNERS
-        return ((y + o // 8) % 4) * 8 + ((l + (o // 4) % 2) % 2) * 4 + (x + o % 4) % 4
+        o = lax.rem(o * STEP, OWNERS)
+        dx = lax.rem(o, 4)
+        dl = lax.rem(lax.div(o, 4), 2)
+        return lax.rem(y + lax.div(o, 8), 4) * 8 + lax.rem(l + dl, 2) * 4 + lax.rem(x + dx, 4)
 
     barrier = pltpu.get_barrier_semaphore()
     for d in range(1, EP):
@@ -97,13 +99,10 @@
 
     def a_pairs(c, k2):
         half = pl.ds((k2 % 2) * HALF, HALF)
-        if c == AUX:
-            return ((mf.at[:, pl.ds(0, 2), half, :], a_bufs[c].at[mine]),)
-        if c == AUX + 1:
-            return (
-                (mf.at[:, pl.ds(2, 1), half, :], a_bufs[c].at[mine, pl.ds(0, 1)]),
-                (hf_rows.at[:, pl.ds(k2, 1)], a_bufs[c].at[mine, pl.ds(1, 1)]),
-            )
+        if c == FACTORS[-1]:
+            return ((hf_rows.at[:, pl.ds(k2, 1)], a_bufs[c].at[mine]),)
+        if c in FACTORS:
+            return ((mf.at[:, pl.ds(c - AUX, 1), half, :], a_bufs[c].at[mine]),)
         b, r0, rows = PIECES[c]
         columns = pl.ds(pl.multiple_of(k2 * COLS + (b % NCB) * BLK, BLK), BLK)
         return ((weights[b // NCB].at[:, pl.ds(r0, rows), columns], a_bufs[c].at[mine]),)
@@ -170,11 +169,11 @@
     def sibling_copies():
         return [
             pltpu.make_async_remote_copy(
-                src_ref=l_bufs[AUX + q].at[:, pl.ds(0, mats)], dst_ref=sibling.at[:, pl.ds(2 * q, mats)],
+                src_ref=l_bufs[AUX + q], dst_ref=sibling.at[:, pl.ds(q, 1)],
                 send_sem=c_send.at[q], recv_sem=c_recv.at[q],
                 device_id=(k + 1 - 2 * core, j), device_id_type=MESH,
             )
-            for q, mats in ((0, 2), (1, 1))
+            for q in range(MATS)
         ]
 
     def b_wait(c):
@@ -184,7 +183,8 @@
         for c, copy in zip(FACTORS, sibling_copies()):
             b_wait(c)
             copy.start()
-        packed = l_bufs[AUX + 1][:, 1].reshape(OWNERS * HALF, BLK)
+        b_wait(FACTORS[-1])
+        packed = l_bufs[FACTORS[-1]][:, 0].reshape(OWNERS * HALF, BLK)
         row = lax.broadcasted_iota(jnp.int32, (RANK, OWNERS * HALF), 0)
         col = lax.broadcasted_iota(jnp.int32, (RANK, OWNERS * HALF), 1)
         row = (row + core * HALF) % RANK
@@ -249,8 +249,8 @@
 
 
 def store(slot_in, blocks, scales, hf_all, sibling, *refs):
-    pieces, aux = refs[: len(LAST_PIECES)], refs[len(LAST_PIECES) : len(LAST_PIECES) + 2]
-    out, scales_out, slot, last, slot_sem, sem = refs[len(LAST_PIECES) + 2 :]
+    pieces, aux = refs[: len(LAST_PIECES)], refs[len(LAST_PIECES) : len(LAST_PIECES + FACTORS)]
+    out, scales_out, slot, last, slot_sem, sem = refs[len(LAST_PIECES + FACTORS) :]
     p, cb = LAST // NCB, LAST % NCB
     copies = []
     fetch = pltpu.make_async_copy(slot_in, slot, slot_sem)
@@ -295,13 +295,13 @@
 def on_device(
     gate_weight, up_weight, down_weight, model_factors, hidden_factors, active, expert_rollout_slot
 ):
-    shapes = [(OWNERS, rows, BLK) for _, _, rows in PIECES] + [(OWNERS, 2, HALF, BLK)] * 2
+    shapes = [(OWNERS, rows, BLK) for _, _, rows in PIECES] + [(OWNERS, 1, HALF, BLK)] * len(FACTORS)
     bufs = [pltpu.VMEM(shape, jnp.bfloat16) for shape in shapes]
     vmem, anywhere = (pl.BlockSpec(memory_space=s) for s in (pltpu.VMEM, pl.ANY))
     sems = pltpu.SemaphoreType.DMA
     n = len(bufs)
 
-    kept = len(LAST_PIECES) + 2
+    kept = len(LAST_PIECES + FACTORS)
     made = pl.pallas_call(
         kernel,
         out_shape=(
@@ -320,7 +320,7 @@
             pltpu.SMEM((LOCAL,), jnp.int32),
             pltpu.SMEM((EXPERTS,), jnp.int32),
             pltpu.SMEM((EXPERTS,), jnp.int32),
-            sems((n,)), sems((n,)), sems((n,)), sems((n,)), sems((2,)), sems((2,)), sems((3,)),
+            sems((n,)), sems((n,)), sems((n,)), sems((n,)), sems((MATS,)), sems((MATS,)), sems((3,)),
         ],
         compiler_params=pltpu.CompilerParams(
             collective_id=0, has_side_effects=True, vmem_limit_bytes=50 * 1024 * 1024

time: 138 us -> 137 us (level)
  no operation moved by 1% of the time
where the time goes in v6:
time: 137 us; the launch traced here: 135 us
  Pallas kernels  135 us (99%)
    pallas_call x1, Pallas kernels, on_device(): pl.pallas_call(kernel, out_shape=(pltpu.VMEM((MATS, OWNERS, BLK, COLS), j...  130 us
    pallas_call x1, Pallas kernels, on_device(): pl.pallas_call(store, out_shape=(jax.ShapeDtypeStruct((MATS, OWNERS, BLK,...  4.74 us

profile of v6, /device:TPU:3, one launch (start us, length us, event | category | flops | bytes accessed | tf_op | source)
XLA Modules:
  0.0 135.4 jit_solution(15584411288791589986)
XLA Ops:
  0.6 0.0 copy-start
  0.6 130.0 %shard_map.86 = (bf16[3,32,128,384]{3,2,1,0:T(8,128)(2,1)S(1)}, f32[3,8,128]{2,1,0:T(8,128)S(1)}, bf16[9,64,128]{2,1,0:T(8,128)(2,1)S(1)}, bf16[32,3,32,128]{3,2...) custom-call(s32[8]{0:T(128)} %active_in.1, ...), custom_call_target="tpu_custom_call" | custom-call | tf_op jit(solution)/shard_map/pallas_call | solution.py:305
  130.7 0.0 copy-done
  130.7 4.7 %shard_map.87 = (bf16[3,32,128,384]{3,2,1,0:T(8,128)(2,1)}, bf16[3,3,32]{2,1,0:T(4,128)(2,1)}) custom-call(s32[32]{0:T(128)S(1)} %copy-done, bf16[3,32,128,384]{3,2,1,0:T(8,128)(2,1)S(1)} %get-tuple-element.15.blocks, f32[3,8,128]{2,1,0:T(8,128)S(1)} %get-tuple-element.16.scales, bf16[9,64,128]{2,1,0:T(8,128)(2,1)S(1)} %get-tuple-element.17.hf_all, ...), custom_call_target="tpu_custom_call" | custom-call | tf_op jit(solution)/shard_map/pallas_call | solution.py:330
Async XLA Ops:
  0.6 130.1 %copy-start = (s32[32]{0:T(128)S(1)}, s32[32]{0:T(128)}, u32[]{:S(2)}) copy-start(s32[32]{0:T(128)} %slot_in.3) | copy-start | bytes 388

commit v7 on v6

--- a/solution.py
+++ b/solution.py
@@ -121,18 +121,16 @@
     def b_start(c):
         a, b, land = a_bufs[c], b_bufs[c], l_bufs[c]
 
-        @pl.loop(0, OWNERS)
-        def _(s):
-            b[s] = a[source[s]]
-
         @pl.loop(1, OWNERS)
         def _(o):
             s = owner(o)
+            b[s] = a[source[s]]
             pltpu.make_async_remote_copy(
                 src_ref=b.at[s], dst_ref=land.at[j], send_sem=b_send.at[c], recv_sem=b_recv.at[c],
                 device_id=(k, s), device_id_type=MESH,
             ).start()
 
+        b[j] = a[source[j]]
         pltpu.make_async_copy(b.at[j], land.at[j], b_recv.at[c]).start()
 
     for c in ORDER[:AUX_AT]:

time: 137 us -> 137 us (level)
  no operation moved by 1% of the time
where the time goes in v7:
time: 137 us; the launch traced here: 135 us
  Pallas kernels  135 us (99%)
    pallas_call x1, Pallas kernels, on_device(): pl.pallas_call(kernel, out_shape=(pltpu.VMEM((MATS, OWNERS, BLK, COLS), j...  130 us
    pallas_call x1, Pallas kernels, on_device(): pl.pallas_call(store, out_shape=(jax.ShapeDtypeStruct((MATS, OWNERS, BLK,...  4.73 us

profile of v7, /device:TPU:3, one launch (start us, length us, event | category | flops | bytes accessed | tf_op | source)
XLA Modules:
  0.0 135.2 jit_solution(1454178332993817784)
XLA Ops:
  0.6 0.0 copy-start
  0.6 129.8 %shard_map.86 = (bf16[3,32,128,384]{3,2,1,0:T(8,128)(2,1)S(1)}, f32[3,8,128]{2,1,0:T(8,128)S(1)}, bf16[9,64,128]{2,1,0:T(8,128)(2,1)S(1)}, bf16[32,3,32,128]{3,2...) custom-call(s32[8]{0:T(128)} %active_in.1, ...), custom_call_target="tpu_custom_call" | custom-call | tf_op jit(solution)/shard_map/pallas_call | solution.py:303
  130.5 0.0 copy-done
  130.5 4.7 %shard_map.87 = (bf16[3,32,128,384]{3,2,1,0:T(8,128)(2,1)}, bf16[3,3,32]{2,1,0:T(4,128)(2,1)}) custom-call(s32[32]{0:T(128)S(1)} %copy-done, bf16[3,32,128,384]{3,2,1,0:T(8,128)(2,1)S(1)} %get-tuple-element.15.blocks, f32[3,8,128]{2,1,0:T(8,128)S(1)} %get-tuple-element.16.scales, bf16[9,64,128]{2,1,0:T(8,128)(2,1)S(1)} %get-tuple-element.17.hf_all, ...), custom_call_target="tpu_custom_call" | custom-call | tf_op jit(solution)/shard_map/pallas_call | solution.py:328
Async XLA Ops:
  0.6 129.9 %copy-start = (s32[32]{0:T(128)S(1)}, s32[32]{0:T(128)}, u32[]{:S(2)}) copy-start(s32[32]{0:T(128)} %slot_in.3) | copy-start | bytes 388
